TPU v7x, 256 devices: a whole 4x4x8 slice. The times are simulated.
256 devices in a mesh: leaf: 64 (over z, x, core), vec: 4 (over y).
Axes of the slice: x: 4, y: 4, z: 8, core: 2. Of those that a mesh axis runs over, the one named last changes fastest.
Arguments:
- vectors: bfloat16 [64, 524288], P('vec', 'leaf'), may hold values from -6 to 6
- points: float32 [3, 524288], P(None, ('leaf', 'vec')), may hold values from 0 to 1
- leaf_basis: bfloat16 [4096, 64, 128], P('leaf'), may hold values from -0.5 to 0.5
- local_transfer: bfloat16 [8192, 64, 64], P('leaf'), may hold values from -0.625 to 0.625
- local_coupling: bfloat16 [8192, 64, 64], P('leaf'), may hold values from -0.75 to 0.75
- upper_transfer: bfloat16 [64, 64, 64], replicated, may hold values from -0.625 to 0.625
- upper_coupling: bfloat16 [64, 64, 64], replicated, may hold values from -0.75 to 0.75
- far_anchor: int32 [16384, 1], P('leaf'), may hold values from 0 to 63; in each aligned block of 256 rows (0 to 255, 256 to 511, ...) at most 8 rows name the same one
- far_leaves: int32 [16384, 2], P('leaf'), may hold values from 0 to 63
- far_block: bfloat16 [16384, 64, 64], P('leaf'), may hold values from -0.5 to 0.5
- near_cols: int32 [4096, 8], P('leaf'), may hold values from 0 to 4095, as said below
Outputs:
- product: float32 [64, 524288], P('vec', 'leaf')
Inputs may be any that keep to these rules, and one draw needn't show every extreme that they name: near_cols[t, 0] = t, and every entry lies within 8 leaves of t. `far_anchor`: among the 256 rows of one index of leaf, no value is named more than 8 times, and in every draw some value is named exactly 8 times.
All inputs are finite; a program needn't handle non-finite values.
Results may differ from a plain program's by a relative error of at most 0.0075.
Values may be sent and summed in bfloat16 or wider, within the bound.
No kernel may reach another device: no remote copies, remote signals or barrier semaphores. Data moves between devices by JAX's collectives and lax.ppermute only.
A program may use at most 128 MiB of HBM per device.

v0:
```python
import jax
import jax.numpy as jnp
from jax import lax
from jax.sharding import PartitionSpec as P

REACH = 8
kernel_scale = 1.0 / 64.0
delta_sq = 0.0025


def swapped(block, axis, distance):
    count = lax.axis_size(axis)
    route = []
    for low in range(count):
        high = low | 1 << distance
        if high != low and high < count:
            route += [(low, high), (high, low)]
    return lax.ppermute(block, axis, route)


def with_halo(cells, sides, width):
    for axis, dim in sides:
        count = lax.axis_size(axis)
        ends = count - 1
        head = lax.slice_in_dim(cells, 0, width, axis=dim)
        tail = lax.slice_in_dim(cells, cells.shape[dim] - width, cells.shape[dim], axis=dim)
        cells = jnp.concatenate(
            [
                lax.ppermute(tail, axis, [(i, (i + 1) % count) for i in range(ends)]),
                cells,
                lax.ppermute(head, axis, [((i + 1) % count, i) for i in range(ends)]),
            ],
            axis=dim,
        )
    return cells


def pick_node(table, node):
    return lax.dynamic_index_in_dim(table, node, 0, keepdims=False)


def per_device(
    vectors,
    points,
    leaf_basis,
    local_transfer,
    local_coupling,
    upper_transfer,
    upper_coupling,
    far_anchor,
    far_leaves,
    far_block,
    near_cols,
):
    highest = lax.Precision.HIGHEST
    vec_cols, point_count = vectors.shape
    leaf_dev, basis_rank, leaf_size = leaf_basis.shape
    n_leaf = lax.axis_size("leaf")
    top_depth = n_leaf.bit_length() - 1
    local_depth = leaf_dev.bit_length() - 1
    device = lax.axis_index("leaf")
    coords = lax.all_gather(points, "vec", axis=1, tiled=True)
    x_leaf = vectors.reshape(vec_cols, leaf_dev, leaf_size)
    coeff = jnp.einsum("vtp,tkp->tvk", x_leaf, leaf_basis, preferred_element_type=jnp.float32)
    transfer = local_transfer.astype(jnp.float32)
    coupling = local_coupling.astype(jnp.float32)
    upper_t = upper_transfer.astype(jnp.float32)
    upper_c = upper_coupling.astype(jnp.float32)
    levels = {local_depth: coeff}
    current = coeff
    for sub_depth in range(local_depth, 0, -1):
        node_count = 2**sub_depth
        product = jnp.einsum(
            "nvk,nkl->nvl", current, transfer[node_count : 2 * node_count], precision=highest
        )
        current = product.reshape(node_count // 2, 2, vec_cols, basis_rank).sum(1)
        levels[sub_depth - 1] = current
    root_coeff = current[0]
    root_share = jnp.dot(root_coeff, transfer[1], precision=highest)
    siblings = []
    carried = jnp.stack([root_coeff, root_share])
    for bit_pos in range(top_depth):
        partner = swapped(carried, "leaf", bit_pos)
        siblings.append(partner[0])
        if bit_pos + 1 < top_depth:
            node = jnp.right_shift(n_leaf + device, bit_pos + 1)
            parent = carried[1] + partner[1]
            carried = jnp.stack(
                [parent, jnp.dot(parent, pick_node(upper_t, node), precision=highest)]
            )
    downward = None
    for tree_depth in range(1, top_depth + 1):
        bit_pos = top_depth - tree_depth
        if bit_pos == 0:
            move_mat = transfer[1]
            pair_mat = coupling[1]
        else:
            node = jnp.right_shift(n_leaf + device, bit_pos)
            move_mat = pick_node(upper_t, node)
            pair_mat = pick_node(upper_c, node)
        coupled = jnp.dot(siblings[bit_pos], pair_mat, precision=highest)
        if downward is None:
            downward = coupled
        else:
            downward = jnp.dot(downward, move_mat.T, precision=highest) + coupled
    downward = downward[None]
    for sub_depth in range(1, local_depth + 1):
        node_count = 2**sub_depth
        coeffs = levels[sub_depth]
        sibling = coeffs.reshape(node_count // 2, 2, vec_cols, basis_rank)[:, ::-1].reshape(
            node_count, vec_cols, basis_rank
        )
        parent = jnp.repeat(downward, 2, axis=0)
        moved = jnp.einsum(
            "nvl,nkl->nvk", parent, transfer[node_count : 2 * node_count], precision=highest
        )
        downward = moved + jnp.einsum(
            "nvk,nkl->nvl", sibling, coupling[node_count : 2 * node_count], precision=highest
        )
    sent = coeff.astype(jnp.bfloat16)
    anchor = far_anchor[:, 0]
    source_local = far_leaves[:, 0]
    target_local = far_leaves[:, 1]
    everything = lax.all_gather(sent, "leaf", axis=0, tiled=True)
    fetched = jnp.take(everything, anchor * leaf_dev + source_local, axis=0)
    contrib = jnp.einsum("pvk,pkl->pvl", fetched, far_block, preferred_element_type=jnp.float32)
    onehot = (target_local[:, None] == jnp.arange(leaf_dev, dtype=jnp.int32)[None, :]).astype(
        jnp.float32
    )
    far_sum = jnp.einsum("pt,pvl->tvl", onehot, contrib, precision=highest)
    leaf_local = (downward + far_sum).astype(jnp.bfloat16)
    far_part = jnp.einsum(
        "tvk,tkp->vtp", leaf_local, leaf_basis, preferred_element_type=jnp.float32
    )
    padded_pts = with_halo(coords.astype(jnp.bfloat16), (("leaf", 1),), REACH * leaf_size).astype(
        coords.dtype
    )
    padded_vec = with_halo(vectors, (("leaf", 1),), REACH * leaf_size)
    block_count = leaf_dev + 2 * REACH
    pts_rows = jnp.transpose(padded_pts.reshape(3, block_count, leaf_size), (1, 0, 2))
    vec_rows = jnp.transpose(padded_vec.reshape(vec_cols, block_count, leaf_size), (1, 0, 2))
    own_rows = jnp.transpose(coords.reshape(3, leaf_dev, leaf_size), (1, 0, 2))
    local_cols = near_cols - device * leaf_dev + REACH
    group_size = min(8, leaf_dev)
    groups = leaf_dev // group_size

    def near_group(group, totals):
        first = group * group_size
        col_ids = lax.dynamic_slice_in_dim(local_cols, first, group_size, 0)
        targets = lax.dynamic_slice_in_dim(own_rows, first, group_size, 0)
        source = jnp.take(pts_rows, col_ids, axis=0)
        delta_x = targets[:, None, 0, :, None] - source[:, :, 0, None, :]
        delta_y = targets[:, None, 1, :, None] - source[:, :, 1, None, :]
        delta_z = targets[:, None, 2, :, None] - source[:, :, 2, None, :]
        dist_sq = delta_x * delta_x + delta_y * delta_y + delta_z * delta_z
        kernel = (kernel_scale * lax.rsqrt(dist_sq + delta_sq)).astype(jnp.bfloat16)
        values = jnp.take(vec_rows, col_ids, axis=0)
        block_sum = jnp.einsum("gkpq,gkvq->vgp", kernel, values, preferred_element_type=jnp.float32)
        return lax.dynamic_update_slice_in_dim(totals, block_sum, first, 1)

    near_sum = lax.fori_loop(
        0, groups, near_group, jnp.zeros((vec_cols, leaf_dev, leaf_size), jnp.float32)
    )
    return (near_sum + far_part).reshape(vec_cols, point_count)


def solution(mesh):
    return jax.shard_map(
        per_device,
        mesh=mesh,
        in_specs=(
            P("vec", "leaf"),
            P(None, ("leaf", "vec")),
            P("leaf", None, None),
            P("leaf", None, None),
            P("leaf", None, None),
            P(),
            P(),
            P("leaf", None),
            P("leaf", None),
            P("leaf", None, None),
            P("leaf", None),
        ),
        out_specs=P("vec", "leaf"),
        check_vma=False,
    )
```

profile of v0, /device:TPU:4, one launch (start us, length us, event | category | flops | bytes accessed | tf_op | source)
XLA Modules:
  0.0 243.2 jit_solution(12452155980335670206)
XLA Ops:
  6.5 2.8 %slice.146 = bf16[64,64,64]{0,2,1:T(8,128)(2,1)} slice(bf16[128,64,64]{0,2,1:T(8,128)(2,1)} %param.16), slice={[64:128], [0:64], [0:64]} | slice | bytes 1048576 | tf_op jit(solution)/shard_map/slice | solution.py:74
  9.3 2.6 %slice.147 = bf16[32,64,64]{0,2,1:T(8,128)(2,1)} slice(bf16[128,64,64]{0,2,1:T(8,128)(2,1)} %param.16), slice={[32:64], [0:64], [0:64]} | slice | bytes 524288 | tf_op jit(solution)/shard_map/slice | solution.py:74
  17.9 2.6 %copy.89 = bf16[64,64,64]{2,1,0:T(8,128)(2,1)S(1)} copy(bf16[64,64,64]{0,2,1:T(8,128)(2,1)} %slice.146) | data formatting | bytes 1048576
  20.5 2.8 %copy.90 = bf16[32,64,64]{2,1,0:T(8,128)(2,1)} copy(bf16[32,64,64]{0,2,1:T(8,128)(2,1)} %slice.147) | data formatting | bytes 524288
  24.6 2.3 copy.92
  26.8 2.4 copy.93
  29.2 2.3 copy.94
  40.1 12.7 %all_gather.6 = f32[3,8192]{1,0:T(4,128)S(1)} all-gather(f32[3,2048]{1,0:T(4,128)} %param.14), channel_id=1, replica_groups=mesh['leaf'=64,'vec'=4] {'vec'}, dimensions={1}, use_global_device_ids=true | all-gather | bytes 122880 | tf_op jit(solution)/shard_map/all_gather | solution.py:62
  56.6 3.6 %collective-permute-start.3 = (bf16[3,1024]{1,0:T(4,128)(2,1)}, bf16[3,1024]{1,0:T(4,128)(2,1)}, u32[]{:S(2)}, u32[]{:S(2)}) collective-permute-start(bf16[3,1024]{1,0:T(4,128)(2,1)} %get-tuple-element.156), channel_id=1, source_target_pairs={{4,0},{8,4},{12,8},{16,12},{20,16},{24,20},{28,24},{32,28},{36,32}... | collective-permute-start | bytes 18440 | tf_op jit(solution)/shard_map/ppermute | solution.py:31
  63.6 3.6 %collective-permute-start.1 = (bf16[16,1024]{1,0:T(8,128)(2,1)}, bf16[16,1024]{1,0:T(8,128)(2,1)}, u32[]{:S(2)}, u32[]{:S(2)}) collective-permute-start(bf16[16,1024]{1,0:T(8,128)(2,1)} %get-tuple-element.154), channel_id=1, source_target_pairs={{4,0},{8,4},{12,8},{16,12},{20,16},{24,20},{28,24},{32,28},{36,32}... | collective-permute-start | bytes 98312 | tf_op jit(solution)/shard_map/ppermute | solution.py:31
  90.5 2.4 copy.96
  92.8 2.3 copy.97
  96.5 2.4 copy.98
  100.3 2.3 copy.99
  105.3 2.8 %copy.101 = bf16[32,64,64]{2,1,0:T(8,128)(2,1)} copy(bf16[32,64,64]{0,2,1:T(8,128)(2,1)} %slice.169) | data formatting | bytes 524288
  108.1 7.5 %copy.83 = bf16[256,64,64]{2,1,0:T(8,128)(2,1)} copy(bf16[256,64,64]{0,2,1:T(8,128)(2,1)} %param.22) | data formatting | bytes 4194304 | tf_op args[9]
  116.4 3.3 %copy.102 = bf16[64,64,64]{2,1,0:T(8,128)(2,1)} copy(bf16[64,64,64]{0,2,1:T(8,128)(2,1)} %slice.170) | data formatting | bytes 1048576
  122.0 6.8 %collective-permute-start.7 = (f32[2,16,64]{2,1,0:T(8,128)S(1)}, f32[2,16,64]{2,1,0:T(8,128)S(1)}, u32[]{:S(2)}, u32[]{:S(2)}) collective-permute-start(f32[2,16,64]{2,1,0:T(8,128)S(1)} %pad_maximum_fusion.3), channel_id=1, source_target_pairs={{0,32},{32,0},{4,36},{36,4},{8,40},{40,8},{12,44},{44,12},{16,48},... | collective-permute-start | bytes 24584 | tf_op jit(solution)/shard_map/ppermute | solution.py:18
  131.7 3.6 %collective-permute-start.8 = (f32[2,16,64]{2,1,0:T(8,128)S(1)}, f32[2,16,64]{2,1,0:T(8,128)S(1)}, u32[]{:S(2)}, u32[]{:S(2)}) collective-permute-start(f32[2,16,64]{2,1,0:T(8,128)S(1)} %pad_maximum_fusion.4), channel_id=1, source_target_pairs={{0,64},{64,0},{4,68},{68,4},{8,72},{72,8},{12,76},{76,12},{16,80},... | collective-permute-start | bytes 24584 | tf_op jit(solution)/shard_map/ppermute | solution.py:18
  138.8 9.0 %collective-permute-start.9 = (f32[2,16,64]{2,1,0:T(8,128)}, f32[2,16,64]{2,1,0:T(8,128)}, u32[]{:S(2)}, u32[]{:S(2)}) collective-permute-start(f32[2,16,64]{2,1,0:T(8,128)} %pad_maximum_fusion.5), channel_id=1, source_target_pairs={{0,128},{128,0},{4,132},{132,4},{8,136},{136,8},{12,140},{140,12},... | collective-permute-start | bytes 24584 | tf_op jit(solution)/shard_map/ppermute | solution.py:18
  148.6 51.6 %while.13 = (s32[]{:T(128)}, f32[16,64,128]{2,0,1:T(8,128)}, s32[64,8]{0,1:T(8,128)S(1)}, bf16[80,16,128]{2,1,0:T(8,128)(2,1)S(1)}, f32[64,3,128]{2,0,1:T(8,128)...) while((s32[]{:T(128)}, f32[16,64,128]{2,0,1:T(8,128)}, ...), condition=%wide.region_1.0_spmd, body=%wide.region_0.0_spmd.sunk | while | flops 45246024 | bytes 1584527 | solution.py:161
  151.7 3.4 %fusion.160 = f32[16,64,128]{2,0,1:T(8,128)} fusion(f32[16,64,128]{2,0,1:T(8,128)} %get-tuple-element.221, s32[]{:T(128)S(6)} %select_n.98, f32[8,8,128]{2,1,0:T(8,128)} %bitcast.277, f32[8,128]{1,0:T(8,128)S(1)} %get-tuple-element.203, f32[8,8,128]{2,1,0:T(8,128)} %bitcast.278, f32[8,128]{1,0:T(8,128)S(1)} %get-tuple-element.205, ...), kind=kOutput, calls=%fused_computation.6.clone.1 | convolution fusion | flops 45219840 | bytes 438340 | tf_op jit(solution)/shard_map/while/body/eval_jaxpr/gkpq,gkvq->vgp/dot_general | solution.py:158
  158.1 3.4 %fusion.160 = f32[16,64,128]{2,0,1:T(8,128)} fusion(f32[16,64,128]{2,0,1:T(8,128)} %get-tuple-element.221, s32[]{:T(128)S(6)} %select_n.98, f32[8,8,128]{2,1,0:T(8,128)} %bitcast.277, f32[8,128]{1,0:T(8,128)S(1)} %get-tuple-element.203, f32[8,8,128]{2,1,0:T(8,128)} %bitcast.278, f32[8,128]{1,0:T(8,128)S(1)} %get-tuple-element.205, ...), kind=kOutput, calls=%fused_computation.6.clone.1 | convolution fusion | flops 45219840 | bytes 438340 | tf_op jit(solution)/shard_map/while/body/eval_jaxpr/gkpq,gkvq->vgp/dot_general | solution.py:158
  164.6 3.4 %fusion.160 = f32[16,64,128]{2,0,1:T(8,128)} fusion(f32[16,64,128]{2,0,1:T(8,128)} %get-tuple-element.221, s32[]{:T(128)S(6)} %select_n.98, f32[8,8,128]{2,1,0:T(8,128)} %bitcast.277, f32[8,128]{1,0:T(8,128)S(1)} %get-tuple-element.203, f32[8,8,128]{2,1,0:T(8,128)} %bitcast.278, f32[8,128]{1,0:T(8,128)S(1)} %get-tuple-element.205, ...), kind=kOutput, calls=%fused_computation.6.clone.1 | convolution fusion | flops 45219840 | bytes 438340 | tf_op jit(solution)/shard_map/while/body/eval_jaxpr/gkpq,gkvq->vgp/dot_general | solution.py:158
  171.0 3.4 %fusion.160 = f32[16,64,128]{2,0,1:T(8,128)} fusion(f32[16,64,128]{2,0,1:T(8,128)} %get-tuple-element.221, s32[]{:T(128)S(6)} %select_n.98, f32[8,8,128]{2,1,0:T(8,128)} %bitcast.277, f32[8,128]{1,0:T(8,128)S(1)} %get-tuple-element.203, f32[8,8,128]{2,1,0:T(8,128)} %bitcast.278, f32[8,128]{1,0:T(8,128)S(1)} %get-tuple-element.205, ...), kind=kOutput, calls=%fused_computation.6.clone.1 | convolution fusion | flops 45219840 | bytes 438340 | tf_op jit(solution)/shard_map/while/body/eval_jaxpr/gkpq,gkvq->vgp/dot_general | solution.py:158
  177.5 3.4 %fusion.160 = f32[16,64,128]{2,0,1:T(8,128)} fusion(f32[16,64,128]{2,0,1:T(8,128)} %get-tuple-element.221, s32[]{:T(128)S(6)} %select_n.98, f32[8,8,128]{2,1,0:T(8,128)} %bitcast.277, f32[8,128]{1,0:T(8,128)S(1)} %get-tuple-element.203, f32[8,8,128]{2,1,0:T(8,128)} %bitcast.278, f32[8,128]{1,0:T(8,128)S(1)} %get-tuple-element.205, ...), kind=kOutput, calls=%fused_computation.6.clone.1 | convolution fusion | flops 45219840 | bytes 438340 | tf_op jit(solution)/shard_map/while/body/eval_jaxpr/gkpq,gkvq->vgp/dot_general | solution.py:158
  184.0 3.4 %fusion.160 = f32[16,64,128]{2,0,1:T(8,128)} fusion(f32[16,64,128]{2,0,1:T(8,128)} %get-tuple-element.221, s32[]{:T(128)S(6)} %select_n.98, f32[8,8,128]{2,1,0:T(8,128)} %bitcast.277, f32[8,128]{1,0:T(8,128)S(1)} %get-tuple-element.203, f32[8,8,128]{2,1,0:T(8,128)} %bitcast.278, f32[8,128]{1,0:T(8,128)S(1)} %get-tuple-element.205, ...), kind=kOutput, calls=%fused_computation.6.clone.1 | convolution fusion | flops 45219840 | bytes 438340 | tf_op jit(solution)/shard_map/while/body/eval_jaxpr/gkpq,gkvq->vgp/dot_general | solution.py:158
  190.4 3.4 %fusion.160 = f32[16,64,128]{2,0,1:T(8,128)} fusion(f32[16,64,128]{2,0,1:T(8,128)} %get-tuple-element.221, s32[]{:T(128)S(6)} %select_n.98, f32[8,8,128]{2,1,0:T(8,128)} %bitcast.277, f32[8,128]{1,0:T(8,128)S(1)} %get-tuple-element.203, f32[8,8,128]{2,1,0:T(8,128)} %bitcast.278, f32[8,128]{1,0:T(8,128)S(1)} %get-tuple-element.205, ...), kind=kOutput, calls=%fused_computation.6.clone.1 | convolution fusion | flops 45219840 | bytes 438340 | tf_op jit(solution)/shard_map/while/body/eval_jaxpr/gkpq,gkvq->vgp/dot_general | solution.py:158
  196.8 3.4 %fusion.160 = f32[16,64,128]{2,0,1:T(8,128)} fusion(f32[16,64,128]{2,0,1:T(8,128)} %get-tuple-element.221, s32[]{:T(128)S(6)} %select_n.98, f32[8,8,128]{2,1,0:T(8,128)} %bitcast.277, f32[8,128]{1,0:T(8,128)S(1)} %get-tuple-element.203, f32[8,8,128]{2,1,0:T(8,128)} %bitcast.278, f32[8,128]{1,0:T(8,128)S(1)} %get-tuple-element.205, ...), kind=kOutput, calls=%fused_computation.6.clone.1 | convolution fusion | flops 45219840 | bytes 438340 | tf_op jit(solution)/shard_map/while/body/eval_jaxpr/gkpq,gkvq->vgp/dot_general | solution.py:158
  219.7 2.5 %fusion.109 = f32[64,16,64]{2,1,0:T(8,128)} fusion(f32[64,16,64]{2,1,0:T(8,128)S(1)} %bitcast.270, bf16[64,64,64]{2,1,0:T(8,128)(2,1)S(1)} %copy.89), kind=kOutput, calls=%fused_computation.160 | convolution fusion | flops 50331648 | bytes 1048576 | tf_op jit(solution)/shard_map/nvl,nkl->nvk/dot_general | solution.py:114
  222.2 6.8 %gather_fusion.2 = bf16[256,16,64]{2,1,0:T(8,128)(2,1)S(1)} fusion(bf16[4096,16,64]{2,1,0:T(8,128)(2,1)} %all-gather.2.cloned.1.call-done, s32[1024]{0:T(1024)} %pad_clamp_fusion.1), kind=kCustom, calls=%fused_computation.2 | custom fusion | bytes 1049600 | tf_op jit(solution)/shard_map/jit(_take)/gather | solution.py:125
  229.0 3.6 %fusion.15 = f32[256,16,64]{2,1,0:T(8,128)S(1)} fusion(bf16[256,64,64]{2,1,0:T(8,128)(2,1)} %copy.83, bf16[256,16,64]{2,1,0:T(8,128)(2,1)S(1)} %gather_fusion.2, pred[256]{0:T(512)(128)(4,1)S(1)} %copy-done.36), kind=kOutput, calls=%fused_computation.40 | convolution fusion | flops 33816576 | bytes 3670272 | tf_op jit(solution)/shard_map/pvk,pkl->pvl/dot_general | solution.py:126
  (268 shorter events, 109.4 us)
Async XLA Ops:
  6.5 26.8 %copy-start = (bf16[64,64,128]{2,1,0:T(8,128)(2,1)S(1)}, bf16[64,64,128]{2,1,0:T(8,128)(2,1)}, u32[]{:S(2)}) copy-start(bf16[64,64,128]{2,1,0:T(8,128)(2,1)} %param.15) | copy-start | bytes 3145732
  6.5 5.4 %copy-start.1 = (bf16[128,64,64]{0,2,1:T(8,128)(2,1)S(1)}, bf16[128,64,64]{0,2,1:T(8,128)(2,1)}, u32[]{:S(2)}) copy-start(bf16[128,64,64]{0,2,1:T(8,128)(2,1)} %param.16) | copy-start | bytes 3145732
  6.5 215.7 %all-gather.2.cloned.1.call-start = ((), (), s32[]{:S(2)}) async-start(), calls=%async_computation | async-start | bytes 17039360 | tf_op jit(solution)/shard_map/all_gather | solution.py:124
  17.9 15.5 %copy-start.13 = (bf16[16,8192]{1,0:T(8,128)(2,1)S(1)}, bf16[16,8192]{1,0:T(8,128)(2,1)}, u32[]{:S(2)}) copy-start(bf16[16,8192]{1,0:T(8,128)(2,1)} %param.13) | copy-start | bytes 786436
  31.5 49.2 %copy-start.2 = (bf16[128,64,64]{0,2,1:T(8,128)(2,1)S(1)}, bf16[128,64,64]{0,2,1:T(8,128)(2,1)}, u32[]{:S(2)}) copy-start(bf16[128,64,64]{0,2,1:T(8,128)(2,1)} %param.17) | copy-start | bytes 3145732
  33.3 48.8 %copy-start.26 = (bf16[1,64,64]{2,1,0:T(8,128)(2,1)}, bf16[1,64,64]{2,1,0:T(8,128)(2,1)S(1)}, u32[]{:S(2)}) copy-start(bf16[1,64,64]{2,1,0:T(8,128)(2,1)S(1)} %copy.95) | copy-start | bytes 24580
  40.1 28.5 %collective-permute-start.4 = (f32[2,16,64]{2,1,0:T(8,128)}, f32[2,16,64]{2,1,0:T(8,128)}, u32[]{:S(2)}, u32[]{:S(2)}) collective-permute-start(f32[2,16,64]{2,1,0:T(8,128)} %pad_maximum_fusion), channel_id=1, source_target_pairs={{0,4},{4,0},{8,12},{12,8},{16,20},{20,16},{24,28},{28,24},{32,36},... | collective-permute-start | bytes 24584 | tf_op jit(solution)/shard_map/ppermute | solution.py:18
  54.7 74.0 %collective-permute-start.2 = (bf16[3,1024]{1,0:T(4,128)(2,1)}, bf16[3,1024]{1,0:T(4,128)(2,1)}, u32[]{:S(2)}, u32[]{:S(2)}) collective-permute-start(bf16[3,1024]{1,0:T(4,128)(2,1)} %get-tuple-element.155), channel_id=1, source_target_pairs={{0,4},{4,8},{8,12},{12,16},{16,20},{20,24},{24,28},{28,32},{32,36}... | collective-permute-start | bytes 18440 | tf_op jit(solution)/shard_map/ppermute | solution.py:29
  56.6 72.1 %collective-permute-start.3 = (bf16[3,1024]{1,0:T(4,128)(2,1)}, bf16[3,1024]{1,0:T(4,128)(2,1)}, u32[]{:S(2)}, u32[]{:S(2)}) collective-permute-start(bf16[3,1024]{1,0:T(4,128)(2,1)} %get-tuple-element.156), channel_id=1, source_target_pairs={{4,0},{8,4},{12,8},{16,12},{20,16},{24,20},{28,24},{32,28},{36,32}... | collective-permute-start | bytes 18440 | tf_op jit(solution)/shard_map/ppermute | solution.py:31
  61.7 73.6 %collective-permute-start = (bf16[16,1024]{1,0:T(8,128)(2,1)}, bf16[16,1024]{1,0:T(8,128)(2,1)}, u32[]{:S(2)}, u32[]{:S(2)}) collective-permute-start(bf16[16,1024]{1,0:T(8,128)(2,1)} %get-tuple-element.153), channel_id=1, source_target_pairs={{0,4},{4,8},{8,12},{12,16},{16,20},{20,24},{24,28},{28,32},{32,36}... | collective-permute-start | bytes 98312 | tf_op jit(solution)/shard_map/ppermute | solution.py:29
  63.6 71.6 %collective-permute-start.1 = (bf16[16,1024]{1,0:T(8,128)(2,1)}, bf16[16,1024]{1,0:T(8,128)(2,1)}, u32[]{:S(2)}, u32[]{:S(2)}) collective-permute-start(bf16[16,1024]{1,0:T(8,128)(2,1)} %get-tuple-element.154), channel_id=1, source_target_pairs={{4,0},{8,4},{12,8},{16,12},{20,16},{24,20},{28,24},{32,28},{36,32}... | collective-permute-start | bytes 98312 | tf_op jit(solution)/shard_map/ppermute | solution.py:31
  71.4 4.1 %collective-permute-start.5 = (f32[2,16,64]{2,1,0:T(8,128)}, f32[2,16,64]{2,1,0:T(8,128)}, u32[]{:S(2)}, u32[]{:S(2)}) collective-permute-start(f32[2,16,64]{2,1,0:T(8,128)} %pad_maximum_fusion.1), channel_id=1, source_target_pairs={{0,8},{8,0},{4,12},{12,4},{16,24},{24,16},{20,28},{28,20},{32,40},... | collective-permute-start | bytes 24584 | tf_op jit(solution)/shard_map/ppermute | solution.py:18
  78.2 42.2 %collective-permute-start.6 = (f32[2,16,64]{2,1,0:T(8,128)}, f32[2,16,64]{2,1,0:T(8,128)}, u32[]{:S(2)}, u32[]{:S(2)}) collective-permute-start(f32[2,16,64]{2,1,0:T(8,128)} %pad_maximum_fusion.2), channel_id=1, source_target_pairs={{0,16},{16,0},{4,20},{20,4},{8,24},{24,8},{12,28},{28,12},{32,48},... | collective-permute-start | bytes 24584 | tf_op jit(solution)/shard_map/ppermute | solution.py:18
  83.5 5.5 %copy-start.35 = (s32[256,2]{0,1:T(2,128)S(1)}, s32[256,2]{0,1:T(2,128)}, u32[]{:S(2)}) copy-start(s32[256,2]{0,1:T(2,128)} %param.21) | copy-start | bytes 6148
  90.5 12.8 %copy-start.7 = (bf16[16,64,64]{0,2,1:T(8,128)(2,1)S(1)}, bf16[16,64,64]{0,2,1:T(8,128)(2,1)}, u32[]{:S(2)}) copy-start(bf16[16,64,64]{0,2,1:T(8,128)(2,1)} %slice.168) | copy-start | bytes 393220
  104.5 11.1 %copy-start.6 = (f32[64,16,64]{2,1,0:T(8,128)S(1)}, f32[64,16,64]{2,1,0:T(8,128)}, u32[]{:S(2)}) copy-start(f32[64,16,64]{2,1,0:T(8,128)} %copy-done.5) | copy-start | bytes 786436
  108.1 11.7 %copy-start.18 = (f32[3,8192]{1,0:T(4,128)S(1)}, f32[3,8192]{1,0:T(4,128)}, u32[]{:S(2)}) copy-start(f32[3,8192]{1,0:T(4,128)} %copy-done.17) | copy-start | bytes 294916
  108.1 12.3 %copy-start.30 = (f32[16,64]{1,0:T(8,128)S(1)}, f32[16,64]{1,0:T(8,128)}, u32[]{:S(2)}) copy-start(f32[16,64]{1,0:T(8,128)} %copy-done.29) | copy-start | bytes 12292
  108.1 20.7 %copy-start.23 = (bf16[3,8192]{1,0:T(4,128)(2,1)S(1)}, bf16[3,8192]{1,0:T(4,128)(2,1)}, u32[]{:S(2)}) copy-start(bf16[3,8192]{1,0:T(4,128)(2,1)} %copy-done.22) | copy-start | bytes 147460
  108.1 27.2 %copy-start.14 = (bf16[16,8192]{1,0:T(8,128)(2,1)S(1)}, bf16[16,8192]{1,0:T(8,128)(2,1)}, u32[]{:S(2)}) copy-start(bf16[16,8192]{1,0:T(8,128)(2,1)} %param.13) | copy-start | bytes 786436
  115.6 33.0 %copy-start.28 = (s32[64,8]{0,1:T(8,128)S(1)}, s32[64,8]{0,1:T(8,128)}, u32[]{:S(2)}) copy-start(s32[64,8]{0,1:T(8,128)} %subtract_add_fusion) | copy-start | bytes 6148
  122.0 8.8 %collective-permute-start.7 = (f32[2,16,64]{2,1,0:T(8,128)S(1)}, f32[2,16,64]{2,1,0:T(8,128)S(1)}, u32[]{:S(2)}, u32[]{:S(2)}) collective-permute-start(f32[2,16,64]{2,1,0:T(8,128)S(1)} %pad_maximum_fusion.3), channel_id=1, source_target_pairs={{0,32},{32,0},{4,36},{36,4},{8,40},{40,8},{12,44},{44,12},{16,48},... | collective-permute-start | bytes 24584 | tf_op jit(solution)/shard_map/ppermute | solution.py:18
  131.7 5.6 %collective-permute-start.8 = (f32[2,16,64]{2,1,0:T(8,128)S(1)}, f32[2,16,64]{2,1,0:T(8,128)S(1)}, u32[]{:S(2)}, u32[]{:S(2)}) collective-permute-start(f32[2,16,64]{2,1,0:T(8,128)S(1)} %pad_maximum_fusion.4), channel_id=1, source_target_pairs={{0,64},{64,0},{4,68},{68,4},{8,72},{72,8},{12,76},{76,12},{16,80},... | collective-permute-start | bytes 24584 | tf_op jit(solution)/shard_map/ppermute | solution.py:18
  137.3 11.3 %copy-start.34 = (f32[2,16,64]{2,1,0:T(8,128)}, f32[2,16,64]{2,1,0:T(8,128)S(1)}, u32[]{:S(2)}) copy-start(f32[2,16,64]{2,1,0:T(8,128)S(1)} %collective-permute-done.8) | copy-start | bytes 24580
  138.8 61.5 %collective-permute-start.9 = (f32[2,16,64]{2,1,0:T(8,128)}, f32[2,16,64]{2,1,0:T(8,128)}, u32[]{:S(2)}, u32[]{:S(2)}) collective-permute-start(f32[2,16,64]{2,1,0:T(8,128)} %pad_maximum_fusion.5), channel_id=1, source_target_pairs={{0,128},{128,0},{4,132},{132,4},{8,136},{136,8},{12,140},{140,12},... | collective-permute-start | bytes 24584 | tf_op jit(solution)/shard_map/ppermute | solution.py:18
  148.6 65.2 %copy-start.16 = (bf16[8,64,64]{2,1,0:T(8,128)(2,1)S(1)}, bf16[8,64,64]{2,1,0:T(8,128)(2,1)}, u32[]{:S(2)}) copy-start(bf16[8,64,64]{2,1,0:T(8,128)(2,1)} %copy.92) | copy-start | bytes 196612
  148.6 69.6 %copy-start.4 = (bf16[32,64,64]{2,1,0:T(8,128)(2,1)S(1)}, bf16[32,64,64]{2,1,0:T(8,128)(2,1)}, u32[]{:S(2)}) copy-start(bf16[32,64,64]{2,1,0:T(8,128)(2,1)} %copy.90) | copy-start | bytes 786436
  200.2 18.9 %copy-start.9 = (bf16[32,64,64]{2,1,0:T(8,128)(2,1)S(1)}, bf16[32,64,64]{2,1,0:T(8,128)(2,1)}, u32[]{:S(2)}) copy-start(bf16[32,64,64]{2,1,0:T(8,128)(2,1)} %copy.101) | copy-start | bytes 786436
  200.2 18.9 %copy-start.19 = (f32[16,2,16,64]{3,2,1,0:T(8,128)S(1)}, f32[16,2,16,64]{3,2,1,0:T(8,128)}, u32[]{:S(2)}) copy-start(f32[16,2,16,64]{3,2,1,0:T(8,128)} %rev.19) | copy-start | bytes 393220
  216.8 12.2 %copy-start.36 = (pred[256]{0:T(512)(128)(4,1)S(1)}, pred[256]{0:T(512)(128)(4,1)}, u32[]{:S(2)}) copy-start(pred[256]{0:T(512)(128)(4,1)} %get-tuple-element.145) | copy-start | bytes 772
  229.0 5.1 %copy-start.8 = (bf16[64,64,64]{2,1,0:T(8,128)(2,1)S(1)}, bf16[64,64,64]{2,1,0:T(8,128)(2,1)}, u32[]{:S(2)}) copy-start(bf16[64,64,64]{2,1,0:T(8,128)(2,1)} %copy.102) | copy-start | bytes 1572868
  229.0 5.1 %copy-start.10 = (f32[32,2,16,64]{3,2,1,0:T(8,128)S(1)}, f32[32,2,16,64]{3,2,1,0:T(8,128)}, u32[]{:S(2)}) copy-start(f32[32,2,16,64]{3,2,1,0:T(8,128)} %rev.20) | copy-start | bytes 786436
  (16 other events, 34.6 us)
Sparse Core Ops, SparseCore 0:
  40.2 101.2 all-gather.1
where the time goes:
time: 247 us; the launch traced here: 243 us
  local copies, waits for them, and re-layouts  106 us (43%)
  matrix products  64.2 us (26%)
  starting transfers between devices  31.6 us (13%)
  between operations  13.8 us (6%)
  blocking collectives  12.7 us (5%)
  other arithmetic  11.6 us (5%)
  waiting for transfers between devices  3.48 us (1%)
    unnamed x91, local copies, waits for them, and re-layouts  44.2 us
    dot_general x8, matrix products, near_group(): jnp.einsum('gkpq,gkvq->vgp', kernel, values, preferred_element_type=jnp.f...  26.8 us
    ppermute x6, starting transfers between devices, swapped(): return lax.ppermute(block, axis, route)  20.5 us
    all_gather x1, blocking collectives, per_device(): coords = lax.all_gather(points, 'vec', axis=1, tiled=True)  12.7 us
    slice x6, local copies, waits for them, and re-layouts, per_device(): transfer[node_count:2 * node_count]  9.92 us
    slice x6, local copies, waits for them, and re-layouts, per_device(): coupling[node_count:2 * node_count]  8.36 us
    ppermute x2, starting transfers between devices, with_halo(): lax.ppermute(head, axis, [((i + 1) % count, i) for i in range(ends)])  7.29 us
    dot_general x6, matrix products, per_device(): jnp.einsum('nvl,nkl->nvk', parent, transfer[node_count:2 * node_count], p...  7.15 us
  transfers between devices with their start and end apart: 11, of which 3 were waited for; matrix products, arithmetic and copies ran while one was open for 54% of the time, Pallas kernels for 0%

commit v1 on v0

--- a/solution.py
+++ b/solution.py
@@ -59,7 +59,9 @@
     top_depth = n_leaf.bit_length() - 1
     local_depth = leaf_dev.bit_length() - 1
     device = lax.axis_index("leaf")
-    coords = lax.all_gather(points, "vec", axis=1, tiled=True)
+    coords = jnp.concatenate(
+        lax.all_to_all(jnp.stack([points] * lax.axis_size("vec")), "vec", 0, 0), axis=1
+    )
     x_leaf = vectors.reshape(vec_cols, leaf_dev, leaf_size)
     coeff = jnp.einsum("vtp,tkp->tvk", x_leaf, leaf_basis, preferred_element_type=jnp.float32)
     transfer = local_transfer.astype(jnp.float32)

time: 247 us -> 221 us (0.89)
  the two profiles are of different devices: /device:TPU:4 before, /device:TPU:111 now
where the time goes in v1:
time: 221 us; the launch traced here: 218 us
  local copies, waits for them, and re-layouts  95.9 us (43%)
  matrix products  54.2 us (25%)
  starting transfers between devices  28.9 us (13%)
  other arithmetic  14 us (6%)
  between operations  13.9 us (6%)
  waiting for transfers between devices  11 us (5%)
    unnamed x88, local copies, waits for them, and re-layouts  44 us
    dot_general x8, matrix products, near_group(): jnp.einsum('gkpq,gkvq->vgp', kernel, values, preferred_element_type=jnp.f...  19.4 us
    ppermute x2, starting transfers between devices, with_halo(): lax.ppermute(tail, axis, [(i, (i + 1) % count) for i in range(ends)])  16.3 us
    slice x6, local copies, waits for them, and re-layouts, per_device(): transfer[node_count:2 * node_count]  9.92 us
    slice x6, local copies, waits for them, and re-layouts, per_device(): coupling[node_count:2 * node_count]  8.4 us
    ppermute x6, waiting for transfers between devices, swapped(): return lax.ppermute(block, axis, route)  7.64 us
    gather x1, local copies, waits for them, and re-layouts, per_device(): fetched = jnp.take(everything, anchor * leaf_dev + source_local, axis=0)  6.76 us
    dot_general x6, matrix products, per_device(): jnp.einsum('nvl,nkl->nvk', parent, transfer[node_count:2 * node_count], p...  6.44 us
  transfers between devices with their start and end apart: 12, of which 4 were waited for; matrix products, arithmetic and copies ran while one was open for 52% of the time, Pallas kernels for 0%

profile of v1, /device:TPU:111, one launch (start us, length us, event | category | flops | bytes accessed | tf_op | source)
XLA Modules:
  0.0 218.3 jit_solution(15885448369726530090)
XLA Ops:
  6.5 2.8 %slice.146 = bf16[64,64,64]{0,2,1:T(8,128)(2,1)} slice(bf16[128,64,64]{0,2,1:T(8,128)(2,1)} %param.16), slice={[64:128], [0:64], [0:64]} | slice | bytes 1048576 | tf_op jit(solution)/shard_map/slice | solution.py:76
  9.3 2.6 %slice.147 = bf16[32,64,64]{0,2,1:T(8,128)(2,1)} slice(bf16[128,64,64]{0,2,1:T(8,128)(2,1)} %param.16), slice={[32:64], [0:64], [0:64]} | slice | bytes 524288 | tf_op jit(solution)/shard_map/slice | solution.py:76
  17.8 2.6 %copy.113 = bf16[64,64,64]{2,1,0:T(8,128)(2,1)S(1)} copy(bf16[64,64,64]{0,2,1:T(8,128)(2,1)} %slice.146) | data formatting | bytes 1048576
  20.5 2.8 %copy.114 = bf16[32,64,64]{2,1,0:T(8,128)(2,1)} copy(bf16[32,64,64]{0,2,1:T(8,128)(2,1)} %slice.147) | data formatting | bytes 524288
  24.5 2.3 %copy.116 = bf16[8,64,64]{2,1,0:T(8,128)(2,1)} copy(bf16[8,64,64]{0,2,1:T(8,128)(2,1)} %slice.149) | data formatting | bytes 131072
  26.8 2.4 %copy.117 = bf16[4,64,64]{2,1,0:T(8,128)(2,1)} copy(bf16[4,64,64]{0,2,1:T(8,128)(2,1)} %slice.150) | data formatting | bytes 65536
  29.2 2.3 %copy.118 = bf16[2,64,64]{2,1,0:T(8,128)(2,1)} copy(bf16[2,64,64]{0,2,1:T(8,128)(2,1)} %slice.151) | data formatting | bytes 32768
  42.2 4.3 %all-to-all-start = ((f32[4,3,2048]{2,1,0:T(4,128)}), f32[4,3,2048]{2,1,0:T(4,128)}, u32[]{:S(2)}, u32[]{:S(2)}) async-start(f32[4,3,2048]{2,1,0:T(4,128)} %stack.58), calls=%async_computation | async-start | bytes 262144 | tf_op jit(solution)/shard_map/all_to_all | solution.py:63
  51.3 6.1 %collective-permute-start = (bf16[16,1024]{1,0:T(8,128)(2,1)}, bf16[16,1024]{1,0:T(8,128)(2,1)}, u32[]{:S(2)}, u32[]{:S(2)}) collective-permute-start(bf16[16,1024]{1,0:T(8,128)(2,1)} %get-tuple-element.159), channel_id=1, source_target_pairs={{0,4},{4,8},{8,12},{12,16},{16,20},{20,24},{24,28},{28,32},{32,36}... | collective-permute-start | bytes 98312 | tf_op jit(solution)/shard_map/ppermute | solution.py:29
  63.4 3.2 %collective-permute-done.6 = f32[2,16,64]{2,1,0:T(8,128)} collective-permute-done((f32[2,16,64]{2,1,0:T(8,128)}, f32[2,16,64]{2,1,0:T(8,128)}, u32[]{:S(2)}, u32[]{:S(2)}) %collective-permute-start.6) | collective-permute-done | bytes 8224 | tf_op jit(solution)/shard_map/ppermute | solution.py:18
  88.4 2.4 %copy.120 = bf16[1,64,64]{2,1,0:T(8,128)(2,1)} copy(bf16[1,64,64]{0,2,1:T(8,128)(2,1)} %slice.164) | data formatting | bytes 16384
  90.7 2.3 %copy.121 = bf16[2,64,64]{2,1,0:T(8,128)(2,1)} copy(bf16[2,64,64]{0,2,1:T(8,128)(2,1)} %slice.165) | data formatting | bytes 32768
  93.6 2.5 %copy.122 = bf16[4,64,64]{2,1,0:T(8,128)(2,1)} copy(bf16[4,64,64]{0,2,1:T(8,128)(2,1)} %slice.166) | data formatting | bytes 65536
  96.7 2.3 %copy.123 = bf16[8,64,64]{2,1,0:T(8,128)(2,1)} copy(bf16[8,64,64]{0,2,1:T(8,128)(2,1)} %slice.167) | data formatting | bytes 131072
  102.7 2.9 %copy.125 = bf16[32,64,64]{2,1,0:T(8,128)(2,1)} copy(bf16[32,64,64]{0,2,1:T(8,128)(2,1)} %slice.169) | data formatting | bytes 524288
  105.6 7.7 %copy.107 = bf16[256,64,64]{2,1,0:T(8,128)(2,1)} copy(bf16[256,64,64]{0,2,1:T(8,128)(2,1)} %param.22) | data formatting | bytes 4194304 | tf_op args[9]
  114.2 3.4 %copy.126 = bf16[64,64,64]{2,1,0:T(8,128)(2,1)} copy(bf16[64,64,64]{0,2,1:T(8,128)(2,1)} %slice.170) | data formatting | bytes 1048576
  119.3 3.0 %collective-permute-start.9 = (f32[2,16,64]{2,1,0:T(8,128)S(1)}, f32[2,16,64]{2,1,0:T(8,128)S(1)}, u32[]{:S(2)}, u32[]{:S(2)}) collective-permute-start(f32[2,16,64]{2,1,0:T(8,128)S(1)} %pad_maximum_fusion.5), channel_id=1, source_target_pairs={{0,128},{128,0},{4,132},{132,4},{8,136},{136,8},{12,140},{140,12},... | collective-permute-start | bytes 24584 | tf_op jit(solution)/shard_map/ppermute | solution.py:18
  123.2 2.9 %collective-permute-done.9 = f32[2,16,64]{2,1,0:T(8,128)S(1)} collective-permute-done((f32[2,16,64]{2,1,0:T(8,128)S(1)}, f32[2,16,64]{2,1,0:T(8,128)S(1)}, u32[]{:S(2)}, u32[]{:S(2)}) %collective-permute-start.9) | collective-permute-done | bytes 8224 | tf_op jit(solution)/shard_map/ppermute | solution.py:18
  144.8 10.2 %collective-permute-start.2 = (bf16[3,1024]{1,0:T(4,128)(2,1)S(1)}, bf16[3,1024]{1,0:T(4,128)(2,1)S(1)}, u32[]{:S(2)}, u32[]{:S(2)}) collective-permute-start(bf16[3,1024]{1,0:T(4,128)(2,1)S(1)} %get-tuple-element.161), channel_id=1, source_target_pairs={{0,4},{4,8},{8,12},{12,16},{16,20},{20,24},{24,28},{28,32},{32,36}... | collective-permute-start | bytes 18440 | tf_op jit(solution)/shard_map/ppermute | solution.py:29
  160.0 3.3 %collective-permute-done.3 = bf16[3,1024]{1,0:T(4,128)(2,1)S(1)} collective-permute-done((bf16[3,1024]{1,0:T(4,128)(2,1)S(1)}, bf16[3,1024]{1,0:T(4,128)(2,1)S(1)}, u32[]{:S(2)}, u32[]{:S(2)}) %collective-permute-start.3) | collective-permute-done | bytes 6176 | tf_op jit(solution)/shard_map/ppermute | solution.py:31
  163.4 33.8 %while.13 = (s32[]{:T(128)}, f32[16,64,128]{2,0,1:T(8,128)S(1)}, s32[64,8]{0,1:T(8,128)S(1)}, bf16[80,16,128]{2,1,0:T(8,128)(2,1)S(1)}, f32[64,3,128]{2,0,1:T(8,...) while((s32[]{:T(128)}, f32[16,64,128]{2,0,1:T(8,128)S(1)}, ...), condition=%wide.region_1.0_spmd, body=%wide.region_0.0_spmd.sunk | while | flops 45246024 | bytes 1585487 | solution.py:163
  165.3 2.4 %fusion.160 = f32[16,64,128]{2,0,1:T(8,128)S(1)} fusion(f32[16,64,128]{2,0,1:T(8,128)S(1)} %get-tuple-element.227, s32[]{:T(128)S(6)} %select_n.98, f32[8,8,128]{2,1,0:T(8,128)S(1)} %bitcast.273, f32[8,128]{1,0:T(8,128)S(1)} %get-tuple-element.209, f32[8,8,128]{2,1,0:T(8,128)S(1)} %bitcast.274, f32[8,128]{1,0:T(8,128)S(1)} %get-tuple-element.211, ...), kind=kOutput, calls=%fused_computation.6.clone.1 | convolution fusion | flops 45219840 | bytes 439300 | tf_op jit(solution)/shard_map/while/body/eval_jaxpr/gkpq,gkvq->vgp/dot_general | solution.py:160
  169.5 2.4 %fusion.160 = f32[16,64,128]{2,0,1:T(8,128)S(1)} fusion(f32[16,64,128]{2,0,1:T(8,128)S(1)} %get-tuple-element.227, s32[]{:T(128)S(6)} %select_n.98, f32[8,8,128]{2,1,0:T(8,128)S(1)} %bitcast.273, f32[8,128]{1,0:T(8,128)S(1)} %get-tuple-element.209, f32[8,8,128]{2,1,0:T(8,128)S(1)} %bitcast.274, f32[8,128]{1,0:T(8,128)S(1)} %get-tuple-element.211, ...), kind=kOutput, calls=%fused_computation.6.clone.1 | convolution fusion | flops 45219840 | bytes 439300 | tf_op jit(solution)/shard_map/while/body/eval_jaxpr/gkpq,gkvq->vgp/dot_general | solution.py:160
  173.7 2.4 %fusion.160 = f32[16,64,128]{2,0,1:T(8,128)S(1)} fusion(f32[16,64,128]{2,0,1:T(8,128)S(1)} %get-tuple-element.227, s32[]{:T(128)S(6)} %select_n.98, f32[8,8,128]{2,1,0:T(8,128)S(1)} %bitcast.273, f32[8,128]{1,0:T(8,128)S(1)} %get-tuple-element.209, f32[8,8,128]{2,1,0:T(8,128)S(1)} %bitcast.274, f32[8,128]{1,0:T(8,128)S(1)} %get-tuple-element.211, ...), kind=kOutput, calls=%fused_computation.6.clone.1 | convolution fusion | flops 45219840 | bytes 439300 | tf_op jit(solution)/shard_map/while/body/eval_jaxpr/gkpq,gkvq->vgp/dot_general | solution.py:160
  177.9 2.4 %fusion.160 = f32[16,64,128]{2,0,1:T(8,128)S(1)} fusion(f32[16,64,128]{2,0,1:T(8,128)S(1)} %get-tuple-element.227, s32[]{:T(128)S(6)} %select_n.98, f32[8,8,128]{2,1,0:T(8,128)S(1)} %bitcast.273, f32[8,128]{1,0:T(8,128)S(1)} %get-tuple-element.209, f32[8,8,128]{2,1,0:T(8,128)S(1)} %bitcast.274, f32[8,128]{1,0:T(8,128)S(1)} %get-tuple-element.211, ...), kind=kOutput, calls=%fused_computation.6.clone.1 | convolution fusion | flops 45219840 | bytes 439300 | tf_op jit(solution)/shard_map/while/body/eval_jaxpr/gkpq,gkvq->vgp/dot_general | solution.py:160
  182.2 2.4 %fusion.160 = f32[16,64,128]{2,0,1:T(8,128)S(1)} fusion(f32[16,64,128]{2,0,1:T(8,128)S(1)} %get-tuple-element.227, s32[]{:T(128)S(6)} %select_n.98, f32[8,8,128]{2,1,0:T(8,128)S(1)} %bitcast.273, f32[8,128]{1,0:T(8,128)S(1)} %get-tuple-element.209, f32[8,8,128]{2,1,0:T(8,128)S(1)} %bitcast.274, f32[8,128]{1,0:T(8,128)S(1)} %get-tuple-element.211, ...), kind=kOutput, calls=%fused_computation.6.clone.1 | convolution fusion | flops 45219840 | bytes 439300 | tf_op jit(solution)/shard_map/while/body/eval_jaxpr/gkpq,gkvq->vgp/dot_general | solution.py:160
  186.4 2.4 %fusion.160 = f32[16,64,128]{2,0,1:T(8,128)S(1)} fusion(f32[16,64,128]{2,0,1:T(8,128)S(1)} %get-tuple-element.227, s32[]{:T(128)S(6)} %select_n.98, f32[8,8,128]{2,1,0:T(8,128)S(1)} %bitcast.273, f32[8,128]{1,0:T(8,128)S(1)} %get-tuple-element.209, f32[8,8,128]{2,1,0:T(8,128)S(1)} %bitcast.274, f32[8,128]{1,0:T(8,128)S(1)} %get-tuple-element.211, ...), kind=kOutput, calls=%fused_computation.6.clone.1 | convolution fusion | flops 45219840 | bytes 439300 | tf_op jit(solution)/shard_map/while/body/eval_jaxpr/gkpq,gkvq->vgp/dot_general | solution.py:160
  190.6 2.4 %fusion.160 = f32[16,64,128]{2,0,1:T(8,128)S(1)} fusion(f32[16,64,128]{2,0,1:T(8,128)S(1)} %get-tuple-element.227, s32[]{:T(128)S(6)} %select_n.98, f32[8,8,128]{2,1,0:T(8,128)S(1)} %bitcast.273, f32[8,128]{1,0:T(8,128)S(1)} %get-tuple-element.209, f32[8,8,128]{2,1,0:T(8,128)S(1)} %bitcast.274, f32[8,128]{1,0:T(8,128)S(1)} %get-tuple-element.211, ...), kind=kOutput, calls=%fused_computation.6.clone.1 | convolution fusion | flops 45219840 | bytes 439300 | tf_op jit(solution)/shard_map/while/body/eval_jaxpr/gkpq,gkvq->vgp/dot_general | solution.py:160
  194.8 2.4 %fusion.160 = f32[16,64,128]{2,0,1:T(8,128)S(1)} fusion(f32[16,64,128]{2,0,1:T(8,128)S(1)} %get-tuple-element.227, s32[]{:T(128)S(6)} %select_n.98, f32[8,8,128]{2,1,0:T(8,128)S(1)} %bitcast.273, f32[8,128]{1,0:T(8,128)S(1)} %get-tuple-element.209, f32[8,8,128]{2,1,0:T(8,128)S(1)} %bitcast.274, f32[8,128]{1,0:T(8,128)S(1)} %get-tuple-element.211, ...), kind=kOutput, calls=%fused_computation.6.clone.1 | convolution fusion | flops 45219840 | bytes 439300 | tf_op jit(solution)/shard_map/while/body/eval_jaxpr/gkpq,gkvq->vgp/dot_general | solution.py:160
  197.3 6.8 %gather_fusion.2 = bf16[256,16,64]{2,1,0:T(8,128)(2,1)S(1)} fusion(bf16[4096,16,64]{2,1,0:T(8,128)(2,1)} %all-gather.2.cloned.1.call-done, s32[1024]{0:T(1024)} %pad_clamp_fusion.1), kind=kCustom, calls=%fused_computation.2 | custom fusion | bytes 1049600 | tf_op jit(solution)/shard_map/jit(_take)/gather | solution.py:127
  204.1 3.6 %fusion.15 = f32[256,16,64]{2,1,0:T(8,128)S(1)} fusion(bf16[256,64,64]{2,1,0:T(8,128)(2,1)} %copy.107, bf16[256,16,64]{2,1,0:T(8,128)(2,1)S(1)} %gather_fusion.2, pred[256]{0:T(512)(128)(4,1)S(1)} %copy-done.35), kind=kOutput, calls=%fused_computation.40 | convolution fusion | flops 33816576 | bytes 3670272 | tf_op jit(solution)/shard_map/pvk,pkl->pvl/dot_general | solution.py:128
  (269 shorter events, 100.0 us)
Async XLA Ops:
  6.5 26.7 %copy-start = (bf16[64,64,128]{2,1,0:T(8,128)(2,1)S(1)}, bf16[64,64,128]{2,1,0:T(8,128)(2,1)}, u32[]{:S(2)}) copy-start(bf16[64,64,128]{2,1,0:T(8,128)(2,1)} %param.15) | copy-start | bytes 3145732
  6.5 5.4 %copy-start.1 = (bf16[128,64,64]{0,2,1:T(8,128)(2,1)S(1)}, bf16[128,64,64]{0,2,1:T(8,128)(2,1)}, u32[]{:S(2)}) copy-start(bf16[128,64,64]{0,2,1:T(8,128)(2,1)} %param.16) | copy-start | bytes 3145732
  6.5 190.7 %all-gather.2.cloned.1.call-start = ((), (), s32[]{:S(2)}) async-start(), calls=%async_computation.1 | async-start | bytes 17039360 | tf_op jit(solution)/shard_map/all_gather | solution.py:126
  17.8 15.4 %copy-start.12 = (bf16[16,8192]{1,0:T(8,128)(2,1)S(1)}, bf16[16,8192]{1,0:T(8,128)(2,1)}, u32[]{:S(2)}) copy-start(bf16[16,8192]{1,0:T(8,128)(2,1)} %param.13) | copy-start | bytes 786436
  31.5 46.5 %copy-start.2 = (bf16[128,64,64]{0,2,1:T(8,128)(2,1)S(1)}, bf16[128,64,64]{0,2,1:T(8,128)(2,1)}, u32[]{:S(2)}) copy-start(bf16[128,64,64]{0,2,1:T(8,128)(2,1)} %param.17) | copy-start | bytes 3145732
  35.6 46.6 %copy-start.9 = (f32[32,16,64]{2,1,0:T(8,128)}, f32[32,16,64]{2,1,0:T(8,128)S(1)}, u32[]{:S(2)}) copy-start(f32[32,16,64]{2,1,0:T(8,128)S(1)} %bitcast_reduce_fusion) | copy-start | bytes 393220
  40.0 6.5 %collective-permute-start.4 = (f32[2,16,64]{2,1,0:T(8,128)}, f32[2,16,64]{2,1,0:T(8,128)}, u32[]{:S(2)}, u32[]{:S(2)}) collective-permute-start(f32[2,16,64]{2,1,0:T(8,128)} %pad_maximum_fusion), channel_id=1, source_target_pairs={{0,4},{4,0},{8,12},{12,8},{16,20},{20,16},{24,28},{28,24},{32,36},... | collective-permute-start | bytes 24584 | tf_op jit(solution)/shard_map/ppermute | solution.py:18
  42.2 101.7 %all-to-all-start = ((f32[4,3,2048]{2,1,0:T(4,128)}), f32[4,3,2048]{2,1,0:T(4,128)}, u32[]{:S(2)}, u32[]{:S(2)}) async-start(f32[4,3,2048]{2,1,0:T(4,128)} %stack.58), calls=%async_computation | async-start | bytes 262144 | tf_op jit(solution)/shard_map/all_to_all | solution.py:63
  49.3 9.9 %collective-permute-start.5 = (f32[2,16,64]{2,1,0:T(8,128)}, f32[2,16,64]{2,1,0:T(8,128)}, u32[]{:S(2)}, u32[]{:S(2)}) collective-permute-start(f32[2,16,64]{2,1,0:T(8,128)} %pad_maximum_fusion.1), channel_id=1, source_target_pairs={{0,8},{8,0},{4,12},{12,4},{16,24},{24,16},{20,28},{28,20},{32,40},... | collective-permute-start | bytes 24584 | tf_op jit(solution)/shard_map/ppermute | solution.py:18
  51.3 71.0 %collective-permute-start = (bf16[16,1024]{1,0:T(8,128)(2,1)}, bf16[16,1024]{1,0:T(8,128)(2,1)}, u32[]{:S(2)}, u32[]{:S(2)}) collective-permute-start(bf16[16,1024]{1,0:T(8,128)(2,1)} %get-tuple-element.159), channel_id=1, source_target_pairs={{0,4},{4,8},{8,12},{12,16},{16,20},{20,24},{24,28},{28,32},{32,36}... | collective-permute-start | bytes 98312 | tf_op jit(solution)/shard_map/ppermute | solution.py:29
  57.3 64.9 %collective-permute-start.1 = (bf16[16,1024]{1,0:T(8,128)(2,1)}, bf16[16,1024]{1,0:T(8,128)(2,1)}, u32[]{:S(2)}, u32[]{:S(2)}) collective-permute-start(bf16[16,1024]{1,0:T(8,128)(2,1)} %get-tuple-element.160), channel_id=1, source_target_pairs={{4,0},{8,4},{12,8},{16,12},{20,16},{24,20},{28,24},{32,28},{36,32}... | collective-permute-start | bytes 98312 | tf_op jit(solution)/shard_map/ppermute | solution.py:31
  62.1 4.5 %collective-permute-start.6 = (f32[2,16,64]{2,1,0:T(8,128)}, f32[2,16,64]{2,1,0:T(8,128)}, u32[]{:S(2)}, u32[]{:S(2)}) collective-permute-start(f32[2,16,64]{2,1,0:T(8,128)} %pad_maximum_fusion.2), channel_id=1, source_target_pairs={{0,16},{16,0},{4,20},{20,4},{8,24},{24,8},{12,28},{28,12},{32,48},... | collective-permute-start | bytes 24584 | tf_op jit(solution)/shard_map/ppermute | solution.py:18
  69.4 3.2 %collective-permute-start.7 = (f32[2,16,64]{2,1,0:T(8,128)}, f32[2,16,64]{2,1,0:T(8,128)}, u32[]{:S(2)}, u32[]{:S(2)}) collective-permute-start(f32[2,16,64]{2,1,0:T(8,128)} %pad_maximum_fusion.3), channel_id=1, source_target_pairs={{0,32},{32,0},{4,36},{36,4},{8,40},{40,8},{12,44},{44,12},{16,48},... | collective-permute-start | bytes 24584 | tf_op jit(solution)/shard_map/ppermute | solution.py:18
  75.4 42.2 %collective-permute-start.8 = (f32[2,16,64]{2,1,0:T(8,128)}, f32[2,16,64]{2,1,0:T(8,128)}, u32[]{:S(2)}, u32[]{:S(2)}) collective-permute-start(f32[2,16,64]{2,1,0:T(8,128)} %pad_maximum_fusion.4), channel_id=1, source_target_pairs={{0,64},{64,0},{4,68},{68,4},{8,72},{72,8},{12,76},{76,12},{16,80},... | collective-permute-start | bytes 24584 | tf_op jit(solution)/shard_map/ppermute | solution.py:18
  80.7 5.7 %copy-start.34 = (s32[256,2]{0,1:T(2,128)S(1)}, s32[256,2]{0,1:T(2,128)}, u32[]{:S(2)}) copy-start(s32[256,2]{0,1:T(2,128)} %param.21) | copy-start | bytes 6148
  83.6 9.4 %copy-start.24 = (f32[4,16,64]{2,1,0:T(8,128)S(1)}, f32[4,16,64]{2,1,0:T(8,128)}, u32[]{:S(2)}) copy-start(f32[4,16,64]{2,1,0:T(8,128)} %copy-done.23) | copy-start | bytes 49156
  85.0 11.1 %copy-start.18 = (f32[8,16,64]{2,1,0:T(8,128)S(1)}, f32[8,16,64]{2,1,0:T(8,128)}, u32[]{:S(2)}) copy-start(f32[8,16,64]{2,1,0:T(8,128)} %copy-done.17) | copy-start | bytes 98308
  88.4 11.3 %copy-start.7 = (bf16[16,64,64]{0,2,1:T(8,128)(2,1)S(1)}, bf16[16,64,64]{0,2,1:T(8,128)(2,1)}, u32[]{:S(2)}) copy-start(bf16[16,64,64]{0,2,1:T(8,128)(2,1)} %slice.168) | copy-start | bytes 393220
  100.9 12.4 %copy-start.6 = (f32[64,16,64]{2,1,0:T(8,128)S(1)}, f32[64,16,64]{2,1,0:T(8,128)}, u32[]{:S(2)}) copy-start(f32[64,16,64]{2,1,0:T(8,128)} %copy-done.5) | copy-start | bytes 786436
  105.6 12.0 %copy-start.28 = (f32[16,64]{1,0:T(8,128)S(1)}, f32[16,64]{1,0:T(8,128)}, u32[]{:S(2)}) copy-start(f32[16,64]{1,0:T(8,128)} %copy-done.27) | copy-start | bytes 12292
  105.6 16.6 %copy-start.13 = (bf16[16,8192]{1,0:T(8,128)(2,1)S(1)}, bf16[16,8192]{1,0:T(8,128)(2,1)}, u32[]{:S(2)}) copy-start(bf16[16,8192]{1,0:T(8,128)(2,1)} %param.13) | copy-start | bytes 786436
  113.3 23.5 %copy-start.20 = (bf16[4,64,64]{2,1,0:T(8,128)(2,1)S(1)}, bf16[4,64,64]{2,1,0:T(8,128)(2,1)}, u32[]{:S(2)}) copy-start(bf16[4,64,64]{2,1,0:T(8,128)(2,1)} %copy.117) | copy-start | bytes 98308
  113.3 29.1 %copy-start.4 = (bf16[32,64,64]{2,1,0:T(8,128)(2,1)S(1)}, bf16[32,64,64]{2,1,0:T(8,128)(2,1)}, u32[]{:S(2)}) copy-start(bf16[32,64,64]{2,1,0:T(8,128)(2,1)} %copy.114) | copy-start | bytes 786436
  114.2 29.2 %copy-start.10 = (bf16[32,64,64]{2,1,0:T(8,128)(2,1)S(1)}, bf16[32,64,64]{2,1,0:T(8,128)(2,1)}, u32[]{:S(2)}) copy-start(bf16[32,64,64]{2,1,0:T(8,128)(2,1)} %copy.125) | copy-start | bytes 786436
  117.6 24.4 %copy-start.16 = (bf16[16,64,64]{2,1,0:T(8,128)(2,1)S(1)}, bf16[16,64,64]{2,1,0:T(8,128)(2,1)}, u32[]{:S(2)}) copy-start(bf16[16,64,64]{2,1,0:T(8,128)(2,1)} %copy.124) | copy-start | bytes 393220
  117.6 24.4 %copy-start.21 = (f32[8,2,16,64]{3,2,1,0:T(8,128)S(1)}, f32[8,2,16,64]{3,2,1,0:T(8,128)}, u32[]{:S(2)}) copy-start(f32[8,2,16,64]{3,2,1,0:T(8,128)} %rev.18) | copy-start | bytes 196612
  117.6 25.7 %copy-start.15 = (f32[16,2,16,64]{3,2,1,0:T(8,128)S(1)}, f32[16,2,16,64]{3,2,1,0:T(8,128)}, u32[]{:S(2)}) copy-start(f32[16,2,16,64]{3,2,1,0:T(8,128)} %rev.19) | copy-start | bytes 393220
  119.3 6.9 %collective-permute-start.9 = (f32[2,16,64]{2,1,0:T(8,128)S(1)}, f32[2,16,64]{2,1,0:T(8,128)S(1)}, u32[]{:S(2)}, u32[]{:S(2)}) collective-permute-start(f32[2,16,64]{2,1,0:T(8,128)S(1)} %pad_maximum_fusion.5), channel_id=1, source_target_pairs={{0,128},{128,0},{4,132},{132,4},{8,136},{136,8},{12,140},{140,12},... | collective-permute-start | bytes 24584 | tf_op jit(solution)/shard_map/ppermute | solution.py:18
  140.5 22.9 %copy-start.26 = (s32[64,8]{0,1:T(8,128)S(1)}, s32[64,8]{0,1:T(8,128)}, u32[]{:S(2)}) copy-start(s32[64,8]{0,1:T(8,128)} %subtract_add_fusion) | copy-start | bytes 6148
  144.8 15.2 %collective-permute-start.2 = (bf16[3,1024]{1,0:T(4,128)(2,1)S(1)}, bf16[3,1024]{1,0:T(4,128)(2,1)S(1)}, u32[]{:S(2)}, u32[]{:S(2)}) collective-permute-start(bf16[3,1024]{1,0:T(4,128)(2,1)S(1)} %get-tuple-element.161), channel_id=1, source_target_pairs={{0,4},{4,8},{8,12},{12,16},{16,20},{20,24},{24,28},{28,32},{32,36}... | collective-permute-start | bytes 18440 | tf_op jit(solution)/shard_map/ppermute | solution.py:29
  155.0 8.3 %collective-permute-start.3 = (bf16[3,1024]{1,0:T(4,128)(2,1)S(1)}, bf16[3,1024]{1,0:T(4,128)(2,1)S(1)}, u32[]{:S(2)}, u32[]{:S(2)}) collective-permute-start(bf16[3,1024]{1,0:T(4,128)(2,1)S(1)} %get-tuple-element.162), channel_id=1, source_target_pairs={{4,0},{8,4},{12,8},{16,12},{20,16},{24,20},{28,24},{32,28},{36,32}... | collective-permute-start | bytes 18440 | tf_op jit(solution)/shard_map/ppermute | solution.py:31
  163.4 40.6 %copy-start.35 = (pred[256]{0:T(512)(128)(4,1)S(1)}, pred[256]{0:T(512)(128)(4,1)}, u32[]{:S(2)}) copy-start(pred[256]{0:T(512)(128)(4,1)} %get-tuple-element.151) | copy-start | bytes 772
  (16 other events, 36.3 us)
Sparse Core Ops, SparseCore 0:
  40.9 99.5 all-gather.1
